TPU v7x, 32 devices: a whole 2x2x4 slice. The times are simulated.
32 devices in a mesh: prow: 4 (over x, core), pcol: 8 (over z, y).
Axes of the slice: x: 2, y: 2, z: 4, core: 2. Of those that a mesh axis runs over, the one named last changes fastest.
Arguments:
- front: float32 [8192, 8192], P('prow', 'pcol'), as said below
- parent_tile: int32 [32], replicated, may hold values from 0 to 31, as said below
Outputs:
- panel_factor: float32 [8192, 1024], P('prow')
- contribution: bfloat16 [8192, 8192], P('prow', 'pcol')
Inputs may be any that keep to these rules, and one draw needn't show every extreme that they name: The front is symmetric positive definite in logical order, with smallest eigenvalue 0.5 or more. parent_tile is a permutation of the 32 tile indices. The tiles whose indices agree modulo 4 go to each such class of parent indices in groups of either none or exactly 2 tiles; tiles whose indices agree modulo 8 go to distinct classes of parent indices modulo 8.
All inputs are finite; a program needn't handle non-finite values.
Results may differ from a plain program's by a relative error of at most 0.001.
Values may be sent and summed in bfloat16 or wider, within the bound.
A program may use at most 192 MiB of HBM per device.

v0:
```python
import jax
import jax.numpy as jnp
from jax import lax
from jax.sharding import PartitionSpec as P

TS = 256
PANELS = 2
PW = 2


def from_root(x, axis, root):
    mine = lax.axis_index(axis) == root
    return lax.psum(jnp.where(mine, x, jnp.zeros_like(x)), axis)


def schur_terms(panel_rows, panel_cols):
    return jnp.einsum("lab,mcb->lamc", panel_rows, panel_cols, precision=lax.Precision.HIGHEST)


def deferred_update(tiles, pending):
    panel_rows, panel_cols, trailing, skipped = pending
    if skipped < 0:
        return tiles - jnp.where(trailing, schur_terms(panel_rows, panel_cols), 0.0)
    other_cols = jnp.concatenate([panel_cols[:skipped], panel_cols[skipped + 1 :]], axis=0)
    other_mask = jnp.concatenate([trailing[:, :, :skipped], trailing[:, :, skipped + 1 :]], axis=2)
    other_tiles = jnp.concatenate([tiles[:, :, :skipped], tiles[:, :, skipped + 1 :]], axis=2)
    updated = other_tiles - jnp.where(other_mask, schur_terms(panel_rows, other_cols), 0.0)
    return jnp.concatenate(
        [updated[:, :, :skipped], tiles[:, :, skipped : skipped + 1], updated], axis=2
    )


def shards(front, parent_tile):
    prows = lax.axis_size("prow")
    pcols = lax.axis_size("pcol")
    row_id = lax.axis_index("prow")
    col_id = lax.axis_index("pcol")
    tile_rows = front.shape[0] // TS
    tile_cols = front.shape[1] // TS
    group = pcols // prows
    steps_total = PANELS * PW
    tiles = front.reshape(tile_rows, TS, tile_cols, TS)
    row_ids = jnp.arange(tile_rows, dtype=jnp.int32) * prows + row_id
    col_ids = jnp.arange(tile_cols, dtype=jnp.int32) * pcols + col_id
    panels = []
    pending = None
    for step in range(steps_total):
        slot_row = step // prows
        slot_col = step // pcols
        pivot_tile = from_root(tiles[slot_row, :, slot_col, :], "prow", step % prows)
        factor = jnp.linalg.cholesky(pivot_tile)
        column = tiles[:, :, slot_col, :]
        right_side = column.reshape(tile_rows * TS, TS).T
        solved = jax.scipy.linalg.solve_triangular(factor, right_side, lower=True).T.reshape(
            tile_rows, TS, TS
        )
        below = (row_ids > step)[:, None, None]
        pivot = (row_ids == step)[:, None, None]
        panel_here = jnp.where(below, solved, jnp.where(pivot, factor[None], 0.0))
        panel_rows = from_root(panel_here, "pcol", step % pcols)
        half = col_id // prows
        picked = lax.dynamic_index_in_dim(
            panel_rows.reshape(tile_cols, group, TS, TS), half, 1, keepdims=False
        )
        panel_cols = from_root(picked, "prow", col_id % prows)
        panels.append(panel_rows)
        trailing = (row_ids > step)[:, None, None, None] & (col_ids > step)[None, None, :, None]
        if pending is not None:
            tiles = deferred_update(tiles, pending)
        if step + 1 < steps_total:
            slot_next = (step + 1) // pcols
            early_part = jnp.einsum(
                "lab,cb->lac", panel_rows, panel_cols[slot_next], precision=lax.Precision.HIGHEST
            )
            tiles = tiles.at[:, :, slot_next, :].add(
                -jnp.where(trailing[:, :, slot_next, :], early_part, 0.0)
            )
            pending = (panel_rows, panel_cols, trailing, slot_next)
        else:
            pending = (panel_rows, panel_cols, trailing, -1)
    tiles = deferred_update(tiles, pending)
    panel_factor = jnp.stack(panels, axis=2).reshape(tile_rows * TS, steps_total * TS)
    keep = (row_ids >= steps_total)[:, None, None, None] & (col_ids >= steps_total)[
        None, None, :, None
    ]
    schur_part = jnp.where(keep, tiles, 0.0).astype(jnp.bfloat16)
    total = parent_tile.shape[0]
    every = jnp.arange(total, dtype=jnp.int32)
    inverse = jnp.sum(jnp.where(parent_tile[None, :] == every[:, None], every[None, :], 0), axis=1)
    row_dest = (parent_tile.reshape(tile_rows, prows) % prows).T
    earlier = jnp.arange(tile_rows)[:, None] > jnp.arange(tile_rows)[None, :]
    alike = row_dest[:, :, None] == row_dest[:, None, :]
    rank = jnp.sum(alike & earlier[None], axis=2)
    slot_of = row_dest * group + rank
    my_slots = lax.dynamic_index_in_dim(slot_of, row_id, 0, keepdims=False)
    row_slots = jnp.arange(prows * group, dtype=jnp.int32)
    send_rows = (row_slots[:, None] == my_slots[None, :]).astype(jnp.bfloat16)
    child_rows = inverse[jnp.arange(tile_rows, dtype=jnp.int32) * prows + row_id]
    source_row = child_rows % prows
    recv_index = source_row * group + rank[source_row, child_rows // prows]
    take_rows = (recv_index[:, None] == row_slots[None, :]).astype(jnp.bfloat16)
    col_dest = parent_tile[col_ids] % pcols
    col_slots = jnp.arange(pcols, dtype=jnp.int32)
    send_cols = (col_slots[:, None] == col_dest[None, :]).astype(jnp.bfloat16)
    child_cols = inverse[jnp.arange(tile_cols, dtype=jnp.int32) * pcols + col_id]
    take_cols = ((child_cols % pcols)[:, None] == col_slots[None, :]).astype(jnp.bfloat16)
    outgoing = jnp.einsum(
        "sl,lamb->samb", send_rows, schur_part, preferred_element_type=jnp.float32
    ).astype(jnp.bfloat16)
    arrived = lax.all_to_all(outgoing, "prow", split_axis=0, concat_axis=0, tiled=True)
    blocks = jnp.einsum(
        "ls,samb->lamb", take_rows, arrived, preferred_element_type=jnp.float32
    ).astype(jnp.bfloat16)
    outgoing = jnp.einsum(
        "em,lamb->elab", send_cols, blocks, preferred_element_type=jnp.float32
    ).astype(jnp.bfloat16)
    move_arrived = lax.all_to_all(outgoing, "pcol", split_axis=0, concat_axis=0, tiled=True)
    moved = jnp.einsum(
        "ns,slab->lanb", take_cols, move_arrived, preferred_element_type=jnp.float32
    ).astype(jnp.bfloat16)
    contribution = moved.reshape(tile_rows * TS, tile_cols * TS)
    return (panel_factor, contribution)


def solution(mesh):
    return jax.shard_map(
        shards,
        mesh=mesh,
        in_specs=(P("prow", "pcol"), P()),
        out_specs=(P("prow", None), P("prow", "pcol")),
        check_vma=False,
    )
```

profile of v0, /device:TPU:0, one launch (start us, length us, event | category | flops | bytes accessed | tf_op | source)
XLA Modules:
  0.0 1334.6 jit_solution(606631405746087958)
XLA Ops:
  29.6 25.3 %all-reduce.14.cloned.1.call-done = f32[256,256]{0,1:T(8,128)} async-done(((f32[256,256]{0,1:T(8,128)}), f32[256,256]{0,1:T(8,128)}) %all-reduce.14.cloned.1.call-update) | async-done | bytes 262160 | tf_op jit(solution)/shard_map/psum | solution.py:13
  79.0 11.7 cholesky.231
  96.9 19.9 %custom-call.20 = f32[2,128,128]{1,2,0:T(8,128)S(1)} custom-call(f32[2,128,128]{2,1,0:T(8,128)S(1)} %get-tuple-element.66), custom_call_target="InvertDiagBlocksLowerTriangular" | custom-call | tf_op jit(solution)/shard_map/jit(_solve_triangular)/triangular_solve | solution.py:54
  135.6 98.2 %all-reduce.16.cloned.1.call-done = f32[8,256,256]{1,2,0:T(8,128)} async-done(((f32[8,256,256]{1,2,0:T(8,128)}), f32[8,256,256]{1,2,0:T(8,128)}) %all-reduce.16.cloned.1.call-update) | async-done | bytes 2097168 | tf_op jit(solution)/shard_map/psum | solution.py:13
  236.7 35.8 %all-reduce.18.cloned.1.call-done = f32[4,256,256]{2,1,0:T(8,128)} async-done(((f32[4,256,256]{2,1,0:T(8,128)}), f32[4,256,256]{2,1,0:T(8,128)}) %all-reduce.18.cloned.1.call-update) | async-done | bytes 1048592 | tf_op jit(solution)/shard_map/psum | solution.py:13
  283.7 27.1 %all-reduce.20.cloned.1.call-done = f32[256,256]{0,1:T(8,128)} async-done(((f32[256,256]{0,1:T(8,128)}), f32[256,256]{0,1:T(8,128)}) %all-reduce.20.cloned.1.call-update) | async-done | bytes 262160 | tf_op jit(solution)/shard_map/psum | solution.py:13
  335.7 11.7 cholesky.265
  353.2 19.8 %custom-call.22 = f32[2,128,128]{1,2,0:T(8,128)S(1)} custom-call(f32[2,128,128]{2,1,0:T(8,128)S(1)} %get-tuple-element.67), custom_call_target="InvertDiagBlocksLowerTriangular" | custom-call | tf_op jit(solution)/shard_map/jit(_solve_triangular)/triangular_solve | solution.py:54
  381.9 101.9 %all-reduce.22.cloned.1.call-done = f32[8,256,256]{1,2,0:T(8,128)} async-done(((f32[8,256,256]{1,2,0:T(8,128)}), f32[8,256,256]{1,2,0:T(8,128)}) %all-reduce.22.cloned.1.call-update) | async-done | bytes 2097168 | tf_op jit(solution)/shard_map/psum | solution.py:13
  486.6 35.8 %all-reduce.24.cloned.1.call-done = f32[4,256,256]{2,1,0:T(8,128)} async-done(((f32[4,256,256]{2,1,0:T(8,128)}), f32[4,256,256]{2,1,0:T(8,128)}) %all-reduce.24.cloned.1.call-update) | async-done | bytes 1048592 | tf_op jit(solution)/shard_map/psum | solution.py:13
  533.5 27.3 %all-reduce.26.cloned.1.call-done = f32[256,256]{0,1:T(8,128)} async-done(((f32[256,256]{0,1:T(8,128)}), f32[256,256]{0,1:T(8,128)}) %all-reduce.26.cloned.1.call-update) | async-done | bytes 262160 | tf_op jit(solution)/shard_map/psum | solution.py:13
  602.9 20.1 %custom-call.24 = f32[2,128,128]{1,2,0:T(8,128)S(1)} custom-call(f32[2,128,128]{2,1,0:T(8,128)S(1)} %get-tuple-element.68), custom_call_target="InvertDiagBlocksLowerTriangular" | custom-call | tf_op jit(solution)/shard_map/jit(_solve_triangular)/triangular_solve | solution.py:54
  631.9 101.9 %all-reduce.28.cloned.1.call-done = f32[8,256,256]{1,2,0:T(8,128)} async-done(((f32[8,256,256]{1,2,0:T(8,128)}), f32[8,256,256]{1,2,0:T(8,128)}) %all-reduce.28.cloned.1.call-update) | async-done | bytes 2097168 | tf_op jit(solution)/shard_map/psum | solution.py:13
  736.6 35.9 %all-reduce.30.cloned.1.call-done = f32[4,256,256]{2,1,0:T(8,128)} async-done(((f32[4,256,256]{2,1,0:T(8,128)}), f32[4,256,256]{2,1,0:T(8,128)}) %all-reduce.30.cloned.1.call-update) | async-done | bytes 1048592 | tf_op jit(solution)/shard_map/psum | solution.py:13
  793.6 17.2 %all-reduce.32.cloned.1.call-done = f32[256,256]{0,1:T(8,128)} async-done(((f32[256,256]{0,1:T(8,128)}), f32[256,256]{0,1:T(8,128)}) %all-reduce.32.cloned.1.call-update) | async-done | bytes 262160 | tf_op jit(solution)/shard_map/psum | solution.py:13
  853.5 19.9 %custom-call.26 = f32[2,128,128]{1,2,0:T(8,128)S(1)} custom-call(f32[2,128,128]{2,1,0:T(8,128)S(1)} %get-tuple-element.69), custom_call_target="InvertDiagBlocksLowerTriangular" | custom-call | tf_op jit(solution)/shard_map/jit(_solve_triangular)/triangular_solve | solution.py:54
  889.7 13.8 %fusion.24 = f32[8,256,3,256]{3,1,2,0:T(8,128)} fusion(f32[8,256,256]{1,2,0:T(8,128)} %all-reduce.16.cloned.1.call-done, f32[4,256,256]{2,1,0:T(8,128)S(1)} %copy-done.10), kind=kOutput, calls=%fused_computation.42 | convolution fusion | flops 4831838208 | bytes 9175040 | tf_op jit(solution)/shard_map/lab,mcb->lamc/dot_general | solution.py:17
  903.4 12.4 fusion.22
  915.8 74.7 %all-reduce.34.cloned.1.call-done = f32[8,256,256]{1,2,0:T(8,128)} async-done(((f32[8,256,256]{1,2,0:T(8,128)}), f32[8,256,256]{1,2,0:T(8,128)}) %all-reduce.34.cloned.1.call-update) | async-done | bytes 2097168 | tf_op jit(solution)/shard_map/psum | solution.py:13
  995.5 20.6 %fusion.5 = f32[8,256,3,256]{3,1,2,0:T(8,128)} fusion(f32[8,256,3,256]{3,2,1,0:T(4,128)} %slice.224, f32[8,256,3,256]{3,1,2,0:T(8,128)} %fusion.22, f32[8,256,3,256]{3,1,2,0:T(8,128)} %fusion.24, pred[8,3]{1,0:T(8,128)(4,1)S(1)} %copy.295, pred[8,3]{1,0:T(8,128)(4,1)S(1)} %copy.293, pred[8,3]{1,0:T(8,128)(4,1)S(1)} %copy.291, ...), kind=kOutput, calls=%fused_computation.21 | convolution fusion | flops 4841275392 | bytes 30146632 | tf_op jit(solution)/shard_map/lab,mcb->lamc/dot_general | solution.py:17
  1019.0 12.4 all-reduce.36.cloned.1.call-done
  1031.4 17.5 %fusion.1 = bf16[8,256,4,256]{3,1,2,0:T(8,128)(2,1)S(1)} fusion(f32[8,256,3,256]{3,1,2,0:T(8,128)} %fusion.5, f32[8,256,1,256]{3,1,2,0:T(8,128)} %copy.297, pred[8,4]{1,0:T(8,128)(4,1)S(1)} %broadcast_and_fusion, pred[8,4]{1,0:T(8,128)(4,1)S(1)} %broadcast_and_fusion.1, f32[8,256,256]{1,2,0:T(8,128)} %all-reduce.34.cloned.1.call-done, ...), kind=kOutput, calls=%fused_computation.15 | convolution fusion | flops 6452936704 | bytes 15728704 | tf_op jit(solution)/shard_map/lab,mcb->lamc/dot_general | solution.py:17
  1062.3 46.1 %all-to-all-done = bf16[8,256,4,256]{3,2,1,0:T(4,128)(2,1)} async-done(((bf16[8,256,4,256]{3,2,1,0:T(4,128)(2,1)}), bf16[8,256,4,256]{3,2,1,0:T(4,128)(2,1)}, u32[]{:S(2)}, u32[]{:S(2)}) %all-to-all-start) | async-done | bytes 4194336 | tf_op jit(solution)/shard_map/all_to_all | solution.py:110
  1157.7 157.9 %all-to-all-done.1 = bf16[8,8,256,256]{3,2,1,0:T(8,128)(2,1)} async-done(((bf16[8,8,256,256]{3,2,1,0:T(8,128)(2,1)}), bf16[8,8,256,256]{3,2,1,0:T(8,128)(2,1)}, u32[]{:S(2)}, u32[]{:S(2)}) %all-to-all-start.1) | async-done | bytes 8388640 | tf_op jit(solution)/shard_map/all_to_all | solution.py:117
  (256 shorter events, 364.6 us)
Async XLA Ops:
  7.2 47.7 %all-reduce.14.cloned.1.call-start = ((), (), s32[]{:S(2)}) async-start(), calls=%async_computation.2 | async-start | bytes 524288 | tf_op jit(solution)/shard_map/psum | solution.py:13
  20.1 213.7 %all-reduce.16.cloned.1.call-start = ((), (), s32[]{:S(2)}) async-start(), calls=%async_computation.3 | async-start | bytes 4194304 | tf_op jit(solution)/shard_map/psum | solution.py:13
  116.8 2.4 copy-start.8
  131.9 140.6 %all-reduce.18.cloned.1.call-start = ((), (), s32[]{:S(2)}) async-start(), calls=%async_computation.4 | async-start | bytes 2097152 | tf_op jit(solution)/shard_map/psum | solution.py:13
  235.4 37.1 %copy-start.2 = (f32[8,256,256]{1,2,0:T(8,128)S(1)}, f32[8,256,256]{1,2,0:T(8,128)}, u32[]{:S(2)}) copy-start(f32[8,256,256]{1,2,0:T(8,128)} %all-reduce.16.cloned.1.call-done) | copy-start | bytes 6291460
  236.5 74.3 %all-reduce.20.cloned.1.call-start = ((), (), s32[]{:S(2)}) async-start(), calls=%async_computation.5 | async-start | bytes 524288 | tf_op jit(solution)/shard_map/psum | solution.py:13
  276.3 1.3 copy-start.7
  278.4 205.3 %all-reduce.22.cloned.1.call-start = ((), (), s32[]{:S(2)}) async-start(), calls=%async_computation.6 | async-start | bytes 4194304 | tf_op jit(solution)/shard_map/psum | solution.py:13
  381.8 140.6 %all-reduce.24.cloned.1.call-start = ((), (), s32[]{:S(2)}) async-start(), calls=%async_computation.7 | async-start | bytes 2097152 | tf_op jit(solution)/shard_map/psum | solution.py:13
  485.4 37.1 %copy-start.3 = (f32[8,256,256]{1,2,0:T(8,128)S(1)}, f32[8,256,256]{1,2,0:T(8,128)}, u32[]{:S(2)}) copy-start(f32[8,256,256]{1,2,0:T(8,128)} %all-reduce.22.cloned.1.call-done) | copy-start | bytes 6291460
  486.5 74.4 %all-reduce.26.cloned.1.call-start = ((), (), s32[]{:S(2)}) async-start(), calls=%async_computation.8 | async-start | bytes 524288 | tf_op jit(solution)/shard_map/psum | solution.py:13
  526.3 1.3 copy-start.6
  528.3 205.4 %all-reduce.28.cloned.1.call-start = ((), (), s32[]{:S(2)}) async-start(), calls=%async_computation.9 | async-start | bytes 4194304 | tf_op jit(solution)/shard_map/psum | solution.py:13
  631.7 140.7 %all-reduce.30.cloned.1.call-start = ((), (), s32[]{:S(2)}) async-start(), calls=%async_computation.10 | async-start | bytes 2097152 | tf_op jit(solution)/shard_map/psum | solution.py:13
  735.4 37.0 %copy-start.1 = (f32[8,256,256]{1,2,0:T(8,128)S(1)}, f32[8,256,256]{1,2,0:T(8,128)}, u32[]{:S(2)}) copy-start(f32[8,256,256]{1,2,0:T(8,128)} %all-reduce.28.cloned.1.call-done) | copy-start | bytes 6291460
  736.5 74.3 %all-reduce.32.cloned.1.call-start = ((), (), s32[]{:S(2)}) async-start(), calls=%async_computation.11 | async-start | bytes 524288 | tf_op jit(solution)/shard_map/psum | solution.py:13
  778.3 212.2 %all-reduce.34.cloned.1.call-start = ((), (), s32[]{:S(2)}) async-start(), calls=%async_computation.12 | async-start | bytes 4194304 | tf_op jit(solution)/shard_map/psum | solution.py:13
  778.4 9.1 copy-start
  873.4 2.4 copy-start.9
  888.5 142.9 %all-reduce.36.cloned.1.call-start = ((), (), s32[]{:S(2)}) async-start(), calls=%async_computation.13 | async-start | bytes 2097152 | tf_op jit(solution)/shard_map/psum | solution.py:13
  889.7 13.8 %copy-start.4 = (f32[8,256,256]{1,2,0:T(8,128)S(1)}, f32[8,256,256]{1,2,0:T(8,128)}, u32[]{:S(2)}) copy-start(f32[8,256,256]{1,2,0:T(8,128)} %all-reduce.22.cloned.1.call-done) | copy-start | bytes 6291460
  889.7 13.8 %copy-start.11 = (f32[4,256,256]{2,1,0:T(8,128)S(1)}, f32[4,256,256]{2,1,0:T(8,128)}, u32[]{:S(2)}) copy-start(f32[4,256,256]{2,1,0:T(8,128)} %all-reduce.24.cloned.1.call-done) | copy-start | bytes 3145732
  1055.1 53.3 %all-to-all-start = ((bf16[8,256,4,256]{3,2,1,0:T(4,128)(2,1)}), bf16[8,256,4,256]{3,2,1,0:T(4,128)(2,1)}, u32[]{:S(2)}, u32[]{:S(2)}) async-start(bf16[8,256,4,256]{3,2,1,0:T(4,128)(2,1)} %copy.301), calls=%async_computation | async-start | bytes 8388608 | tf_op jit(solution)/shard_map/all_to_all | solution.py:110
  1127.1 188.5 %all-to-all-start.1 = ((bf16[8,8,256,256]{3,2,1,0:T(8,128)(2,1)}), bf16[8,8,256,256]{3,2,1,0:T(8,128)(2,1)}, u32[]{:S(2)}, u32[]{:S(2)}) async-start(bf16[8,8,256,256]{3,2,1,0:T(8,128)(2,1)} %copy.304), calls=%async_computation.1 | async-start | bytes 16777216 | tf_op jit(solution)/shard_map/all_to_all | solution.py:117
  (2 other events, 2.5 us)
Sparse Core Ops, SparseCore 0:
  20.2 34.6 all-reduce.13
  132.0 101.7 all-reduce.15
  236.7 35.7 all-reduce.17
  278.5 32.3 all-reduce.19
  381.9 101.7 all-reduce.21
  486.6 35.7 all-reduce.23
  528.5 32.3 all-reduce.25
  631.8 101.8 all-reduce.27
  736.6 35.7 all-reduce.29
  778.4 32.3 all-reduce.31
  888.6 101.8 all-reduce.33
  995.6 35.7 all-reduce.35
where the time goes:
time: 1340 us; the launch traced here: 1330 us
  waiting for transfers between devices  798 us (60%)
  other arithmetic  248 us (19%)
  local copies, waits for them, and re-layouts  143 us (11%)
  matrix products  114 us (9%)
  between operations  20.2 us (2%)
    psum x12, waiting for transfers between devices, from_root(): return lax.psum(jnp.where(mine, x, jnp.zeros_like(x)), axis)  593 us
    all_to_all x1, waiting for transfers between devices, shards(): lax.all_to_all(outgoing, 'pcol', split_axis=0, concat_axis=0, tiled=True)  158 us
    another operation x27, other arithmetic, shards(): factor = jnp.linalg.cholesky(pivot_tile)  138 us
    another operation x9, other arithmetic, shards(): jax.scipy.linalg.solve_triangular(factor, right_side, lower=True)  79.8 us
    dot_general x4, matrix products, schur_terms(): jnp.einsum('lab,mcb->lamc', panel_rows, panel_cols, precision=lax.Precisi...  64.3 us
    all_to_all x1, waiting for transfers between devices, shards(): lax.all_to_all(outgoing, 'prow', split_axis=0, concat_axis=0, tiled=True)  46.1 us
    unnamed x33, local copies, waits for them, and re-layouts  32.8 us
  transfers between devices with their start and end apart: 14, of which 14 were waited for; matrix products, arithmetic and copies ran while one was open for 9% of the time, Pallas kernels for 0%

commit v1 on v0

v1 whole, which is shorter than its diff:
```python
import jax
import jax.numpy as jnp
from jax import lax
from jax.experimental import pallas as pl
from jax.experimental.pallas import tpu as pltpu
from jax.sharding import PartitionSpec as P

TS = 256
PANELS = 2
PW = 2
BLOCK = 128
FULL = lax.Precision.HIGHEST


def eliminate(block):
    lane = lax.broadcasted_iota(jnp.int32, (BLOCK, BLOCK), 1)
    sub = lax.broadcasted_iota(jnp.int32, (BLOCK, BLOCK), 0)
    done = []
    rest = block
    for j in range(BLOCK):
        first = (j // 8) * 8
        here = j - first
        row = rest[here : here + 1, :]
        pivot = rest[here : here + 1, j : j + 1]
        scale = 1.0 / pivot
        at = lane[:1] == j
        pivot_row = jnp.where(at, 1.0, row) * scale
        factors = jnp.where(sub[first:] > j, rest[:, j : j + 1], 0.0)
        cleared = jnp.where((lane[first:] == j) & (sub[first:] > j), 0.0, rest)
        rest = cleared - factors * pivot_row
        if here == 7:
            done.append(rest[:8])
            rest = rest[8:]
    full = jnp.concatenate(done, axis=0)
    diagonal = jnp.sum(jnp.where(lane == sub, full, 0.0), axis=1, keepdims=True)
    root = lax.rsqrt(diagonal)
    upper = jnp.where(lane >= sub, full, 0.0) * root
    inverse = jnp.where(lane < sub, full, jnp.where(lane == sub, 1.0, 0.0)) * root
    return upper, inverse


def factor_kernel(front_ref, inverse_ref, work, panel):
    order = front_ref.shape[0]
    blocks = order // BLOCK
    work[...] = front_ref[...]
    inverse_ref[...] = jnp.where(
        lax.broadcasted_iota(jnp.int32, (order, order), 0)
        == lax.broadcasted_iota(jnp.int32, (order, order), 1),
        1.0,
        0.0,
    )

    @pl.loop(0, blocks)
    def _(k):
        start = pl.multiple_of(k * BLOCK, BLOCK)
        rows = pl.ds(start, BLOCK)
        _, inverse = eliminate(work[rows, rows])
        lanes = lax.broadcasted_iota(jnp.int32, (BLOCK, order), 1)
        top = jnp.dot(inverse, work[rows, :], precision=FULL, preferred_element_type=jnp.float32)
        panel[...] = jnp.where(lanes >= start + BLOCK, top, 0.0)
        inverse_ref[rows, :] = jnp.dot(
            inverse, inverse_ref[rows, :], precision=FULL, preferred_element_type=jnp.float32
        )

        @pl.loop(k + 1, blocks)
        def _(i):
            below = pl.ds(pl.multiple_of(i * BLOCK, BLOCK), BLOCK)
            left = panel[:, below].T
            work[below, :] -= jnp.dot(
                left, panel[...], precision=FULL, preferred_element_type=jnp.float32
            )
            inverse_ref[below, :] -= jnp.dot(
                left, inverse_ref[rows, :], precision=FULL, preferred_element_type=jnp.float32
            )


def inverse_factor(leading):
    order = leading.shape[0]
    return pl.pallas_call(
        factor_kernel,
        out_shape=jax.ShapeDtypeStruct((order, order), jnp.float32),
        in_specs=[pl.BlockSpec(memory_space=pltpu.VMEM)],
        out_specs=pl.BlockSpec(memory_space=pltpu.VMEM),
        scratch_shapes=[
            pltpu.VMEM((order, order), jnp.float32),
            pltpu.VMEM((BLOCK, order), jnp.float32),
        ],
        compiler_params=pltpu.CompilerParams(vmem_limit_bytes=32 * 1024 * 1024),
        cost_estimate=pl.CostEstimate(
            flops=20 * order**3, bytes_accessed=8 * order**2, transcendentals=0
        ),
    )(leading)


def panel_rows(front, prows, pcols, steps):
    tile_rows = front.shape[0] // TS
    tile_cols = front.shape[1] // TS
    group = pcols // prows
    col_id = lax.axis_index("pcol")
    pairs = [
        (k * pcols + g * prows + s, s * pcols + g * prows + k)
        for g in range(1, group)
        for k in range(prows)
        for s in range(prows)
    ]
    swapped = lax.ppermute(front[:TS], ("prow", "pcol"), pairs)
    swapped = swapped.T.reshape(tile_cols, TS, TS)
    native = front[:, :TS].reshape(tile_cols, group, TS, TS)[:, 0]
    mine = jnp.where(col_id < prows, native, swapped)
    every = lax.all_gather(mine, "pcol", axis=0, tiled=False)
    every = every.reshape(group, prows, tile_cols, TS, TS)[:, :steps]
    return every.transpose(2, 0, 3, 1, 4).reshape(tile_rows * TS, steps * TS)


def shards(front, parent_tile):
    prows = lax.axis_size("prow")
    pcols = lax.axis_size("pcol")
    row_id = lax.axis_index("prow")
    col_id = lax.axis_index("pcol")
    tile_rows = front.shape[0] // TS
    tile_cols = front.shape[1] // TS
    group = pcols // prows
    steps_total = PANELS * PW
    width = steps_total * TS
    assert steps_total <= prows and group * prows == pcols

    corner = lax.all_gather(front[:TS, :TS], "pcol", axis=0, tiled=False)[:steps_total]
    corner = corner.transpose(1, 0, 2).reshape(TS, width)
    strips = lax.all_gather(jnp.concatenate([corner, front[:TS]], axis=1), "prow", axis=0, tiled=True)
    strips = strips[:width]
    leading, front_cols = strips[:, :width], strips[:, width:]
    front_rows = panel_rows(front, prows, pcols, steps_total)

    inverse_low = inverse_factor(leading)
    factor_cols = jnp.dot(inverse_low, front_cols, precision=lax.Precision.HIGH)
    factor_rows = lax.dot_general(
        front_rows, inverse_low, (((1,), (1,)), ((), ())), precision=lax.Precision.HIGH
    )
    local = jnp.arange(tile_rows * TS, dtype=jnp.int32)
    row_pos = (local // TS * prows + row_id) * TS + local % TS
    panel_factor = jnp.where(
        row_pos[:, None] >= jnp.arange(width, dtype=jnp.int32)[None, :], factor_rows, 0.0
    )

    row_ids = jnp.arange(tile_rows, dtype=jnp.int32) * prows + row_id
    col_ids = jnp.arange(tile_cols, dtype=jnp.int32) * pcols + col_id
    keep = (row_ids >= steps_total)[:, None, None, None] & (col_ids >= steps_total)[
        None, None, :, None
    ]
    remaining = front - jnp.dot(panel_factor, factor_cols, precision=lax.Precision.HIGH)
    remaining = remaining.reshape(tile_rows, TS, tile_cols, TS)
    schur_part = jnp.where(keep, remaining, 0.0).astype(jnp.bfloat16)

    total = parent_tile.shape[0]
    every = jnp.arange(total, dtype=jnp.int32)
    inverse = jnp.sum(jnp.where(parent_tile[None, :] == every[:, None], every[None, :], 0), axis=1)
    row_dest = (parent_tile.reshape(tile_rows, prows) % prows).T
    earlier = jnp.arange(tile_rows)[:, None] > jnp.arange(tile_rows)[None, :]
    alike = row_dest[:, :, None] == row_dest[:, None, :]
    rank = jnp.sum(alike & earlier[None], axis=2)
    slot_of = row_dest * group + rank
    my_slots = lax.dynamic_index_in_dim(slot_of, row_id, 0, keepdims=False)
    row_slots = jnp.arange(prows * group, dtype=jnp.int32)
    send_rows = (row_slots[:, None] == my_slots[None, :]).astype(jnp.bfloat16)
    child_rows = inverse[jnp.arange(tile_rows, dtype=jnp.int32) * prows + row_id]
    source_row = child_rows % prows
    recv_index = source_row * group + rank[source_row, child_rows // prows]
    take_rows = (recv_index[:, None] == row_slots[None, :]).astype(jnp.bfloat16)
    col_dest = parent_tile[col_ids] % pcols
    col_slots = jnp.arange(pcols, dtype=jnp.int32)
    send_cols = (col_slots[:, None] == col_dest[None, :]).astype(jnp.bfloat16)
    child_cols = inverse[jnp.arange(tile_cols, dtype=jnp.int32) * pcols + col_id]
    take_cols = ((child_cols % pcols)[:, None] == col_slots[None, :]).astype(jnp.bfloat16)
    outgoing = jnp.einsum(
        "sl,lamb->samb", send_rows, schur_part, preferred_element_type=jnp.float32
    ).astype(jnp.bfloat16)
    arrived = lax.all_to_all(outgoing, "prow", split_axis=0, concat_axis=0, tiled=True)
    blocks = jnp.einsum(
        "ls,samb->lamb", take_rows, arrived, preferred_element_type=jnp.float32
    ).astype(jnp.bfloat16)
    outgoing = jnp.einsum(
        "em,lamb->elab", send_cols, blocks, preferred_element_type=jnp.float32
    ).astype(jnp.bfloat16)
    move_arrived = lax.all_to_all(outgoing, "pcol", split_axis=0, concat_axis=0, tiled=True)
    moved = jnp.einsum(
        "ns,slab->lanb", take_cols, move_arrived, preferred_element_type=jnp.float32
    ).astype(jnp.bfloat16)
    contribution = moved.reshape(tile_rows * TS, tile_cols * TS)
    return (panel_factor, contribution)


def solution(mesh):
    return jax.shard_map(
        shards,
        mesh=mesh,
        in_specs=(P("prow", "pcol"), P()),
        out_specs=(P("prow", None), P("prow", "pcol")),
        check_vma=False,
    )
```

time: 1340 us -> 725 us (0.54)
  waiting for transfers between devices: 798 us -> 441 us
  other arithmetic: 248 us -> 3.11 us
  Pallas kernels: 0 us -> 124 us
  local copies, waits for them, and re-layouts: 143 us -> 57.8 us
  matrix products: 114 us -> 64 us
    psum x12 -> x0, waiting for transfers between devices: 593 us -> none  [from_root(): return lax.psum(jnp.where(mine, x, jnp.zeros_like(x)), axis)]
    another operation x37 -> x0, other arithmetic: 223 us -> none  [the longest x27 138 us: shards(): factor = jnp.linalg.cholesky(pivot_tile)]
    all_gather x0 -> x3, waiting for transfers between devices: none -> 213 us  [the longest x1 123 us: panel_rows(): every = lax.all_gather(mine, 'pcol', axis=0, tiled=False)]
    pallas_call x0 -> x1, Pallas kernels: none -> 124 us  [inverse_factor(): pl.pallas_call(factor_kernel, out_shape=jax.ShapeDtypeStruct((order, orde...]
    dot_general x7 -> x3, matrix products: 75.8 us -> 40.1 us  [the longest x1 15.7 us: shards(): lax.dot_general(front_rows, inverse_low, (((1,), (1,)), ((), ())), precis...]
    another operation x41 -> x0, local copies, waits for them, and re-layouts: 25.1 us -> none  [the longest x29 15.1 us: shards(): jax.scipy.linalg.solve_triangular(factor, right_side, lower=True)]
    all_to_all x1, waiting for transfers between devices: 158 us -> 182 us  [shards(): lax.all_to_all(outgoing, 'pcol', split_axis=0, concat_axis=0, tiled=True)]
    unnamed x33 -> x19, local copies, waits for them, and re-layouts: 32.8 us -> 12 us
  transfers between devices with their start and end apart: 14 -> 6, of which waited for: 14 -> 5; matrix products, arithmetic and copies ran while one was open for 9% -> 5% of each run, Pallas kernels for 0% -> 0%
where the time goes in v1:
time: 725 us; the launch traced here: 717 us
  waiting for transfers between devices  441 us (61%)
  Pallas kernels  124 us (17%)
  matrix products  64 us (9%)
  local copies, waits for them, and re-layouts  57.8 us (8%)
  between operations  14.5 us (2%)
  starting transfers between devices  12.5 us (2%)
    all_to_all x1, waiting for transfers between devices, shards(): lax.all_to_all(outgoing, 'pcol', split_axis=0, concat_axis=0, tiled=True)  182 us
    pallas_call x1, Pallas kernels, inverse_factor(): pl.pallas_call(factor_kernel, out_shape=jax.ShapeDtypeStruct((order, orde...  124 us
    all_gather x1, waiting for transfers between devices, panel_rows(): every = lax.all_gather(mine, 'pcol', axis=0, tiled=False)  123 us
    all_gather x1, waiting for transfers between devices, shards(): lax.all_gather(front[:TS, :TS], 'pcol', axis=0, tiled=False)[:steps_total]  52.7 us
    all_to_all x1, waiting for transfers between devices, shards(): lax.all_to_all(outgoing, 'prow', split_axis=0, concat_axis=0, tiled=True)  46.1 us
    all_gather x1, waiting for transfers between devices, shards(): lax.all_gather(jnp.concatenate([corner, front[:TS]], axis=1), 'prow', axi...  36.7 us
    dot_general x1, matrix products, shards(): lax.dot_general(front_rows, inverse_low, (((1,), (1,)), ((), ())), precis...  15.7 us
    dot_general x1, matrix products, shards(): jnp.dot(panel_factor, factor_cols, precision=lax.Precision.HIGH)  14.9 us
  transfers between devices with their start and end apart: 6, of which 5 were waited for; matrix products, arithmetic and copies ran while one was open for 5% of the time, Pallas kernels for 0%

profile of v1, /device:TPU:0, one launch (start us, length us, event | category | flops | bytes accessed | tf_op | source)
XLA Modules:
  0.0 717.0 jit_solution(15406350335568316286)
XLA Ops:
  7.2 1.7 slice.25
  10.4 1.7 collective-permute-start
  14.9 52.7 %all-gather.9.cloned.1.call-done = f32[2048,256]{1,0:T(8,128)} async-done(((f32[256,256]{1,0:T(8,128)}), f32[2048,256]{1,0:T(8,128)}) %all-gather.9.cloned.1.call-update) | async-done | bytes 2097168 | tf_op jit(solution)/shard_map/all_gather | solution.py:127
  71.9 123.4 %all-gather.5.cloned.1.call-done = f32[8,4,256,256]{3,2,1,0:T(8,128)} async-done(((f32[1,4,256,256]{3,2,1,0:T(8,128)}), f32[8,4,256,256]{3,2,1,0:T(8,128)}) %all-gather.5.cloned.1.call-update) | async-done | bytes 8388624 | tf_op jit(solution)/shard_map/all_gather | solution.py:110
  195.3 13.2 %copy.51 = f32[4,2,256,4,256]{4,3,2,1,0:T(4,128)} copy(f32[4,2,256,4,256]{4,2,0,3,1:T(8,128)} %bitcast.75) | data formatting | bytes 16777216 | tf_op jit(solution)/shard_map/transpose | solution.py:112
  208.5 8.7 %copy.67 = f32[256,8,4,256]{3,1,2,0:T(8,128)} copy(f32[256,8,4,256]{3,2,1,0:T(4,128)} %bitcast.73) | data formatting | bytes 16777216
  217.2 36.7 %all-gather.7.cloned.1.call-done = f32[1024,2048]{1,0:T(8,128)} async-done(((f32[256,2048]{1,0:T(8,128)}), f32[1024,2048]{1,0:T(8,128)}) %all-gather.7.cloned.1.call-update) | async-done | bytes 8388624 | tf_op jit(solution)/shard_map/all_gather | solution.py:129
  253.9 2.9 slice.40.front_ref
  256.9 123.8 %shard_map.41 = f32[1024,1024]{1,0:T(8,128)S(1)} custom-call(f32[1024,1024]{1,0:T(8,128)S(1)} %slice.40.front_ref), custom_call_target="tpu_custom_call" | custom-call | flops 21474836480 | bytes 8388608 | tf_op jit(solution)/shard_map/pallas_call | solution.py:79
  380.7 15.7 %fusion.3 = f32[2048,1024]{1,0:T(8,128)} fusion(s32[2048]{0:T(1024)S(1)} %fusion.32, f32[2048,1024]{1,0:T(8,128)S(1)} %bitcast.78, f32[1024,1024]{1,0:T(8,128)S(1)} %shard_map.41), kind=kOutput, calls=%fused_computation.9 | convolution fusion | flops 12889096192 | bytes 20979712 | tf_op jit(solution)/shard_map/dot_general | solution.py:136
  396.5 9.5 %fusion.9 = f32[1024,1024]{1,0:T(8,128)S(1)} fusion(f32[1024,1024]{1,0:T(8,128)S(1)} %shard_map.41, f32[1024,2048]{1,0:T(8,128)} %all-gather.7.cloned.1.call-done), kind=kOutput, calls=%fused_computation.13 | convolution fusion | flops 6442450944 | bytes 12582912 | tf_op jit(solution)/shard_map/dot_general | solution.py:135
  406.0 14.9 %convolution_subtract_fusion = bf16[2048,1024]{1,0:T(8,128)(2,1)} fusion(f32[2048,1024]{1,0:T(8,128)S(1)} %bitcast.80, f32[2048,1024]{1,0:T(8,128)S(1)} %copy-done.3, f32[1024,1024]{1,0:T(8,128)S(1)} %fusion.9), kind=kOutput, calls=%fused_computation.20 | convolution fusion | flops 12889096192 | bytes 25165824 | tf_op jit(solution)/shard_map/dot_general | solution.py:150
  420.9 8.0 %reshape.295 = bf16[8,256,4,256]{3,2,1,0:T(4,128)(2,1)} reshape(bf16[2048,1024]{1,0:T(8,128)(2,1)} %convolution_subtract_fusion) | data formatting | bytes 8388608 | tf_op jit(solution)/shard_map/reshape | solution.py:151
  428.9 4.7 fusion.19
  433.7 3.6 copy.57
  437.3 4.9 all-to-all-start
  444.4 46.1 %all-to-all-done = bf16[8,256,4,256]{3,2,1,0:T(4,128)(2,1)} async-done(((bf16[8,256,4,256]{3,2,1,0:T(4,128)(2,1)}), bf16[8,256,4,256]{3,2,1,0:T(4,128)(2,1)}, u32[]{:S(2)}, u32[]{:S(2)}) %all-to-all-start) | async-done | bytes 4194336 | tf_op jit(solution)/shard_map/all_to_all | solution.py:177
  490.4 4.7 fusion.16
  495.2 5.6 convolution_convert_fusion
  500.7 8.6 %copy.60 = bf16[8,8,256,256]{3,2,1,0:T(8,128)(2,1)} copy(bf16[8,8,256,256]{3,0,2,1:T(8,128)(2,1)} %convolution_convert_fusion) | data formatting | bytes 16777216 | tf_op jit(solution)/shard_map/convert_element_type | solution.py:183
  509.4 5.8 all-to-all-start.1
  515.9 182.2 %all-to-all-done.1 = bf16[8,8,256,256]{3,2,1,0:T(8,128)(2,1)} async-done(((bf16[8,8,256,256]{3,2,1,0:T(8,128)(2,1)}), bf16[8,8,256,256]{3,2,1,0:T(8,128)(2,1)}, u32[]{:S(2)}, u32[]{:S(2)}) %all-to-all-start.1) | async-done | bytes 8388640 | tf_op jit(solution)/shard_map/all_to_all | solution.py:184
  698.1 8.9 %fusion.4 = bf16[8,256,256,4]{2,3,1,0:T(4,128)(2,1)S(1)} fusion(bf16[8,8,256,256]{3,2,1,0:T(8,128)(2,1)} %all-to-all-done.1, s32[4]{0:T(128)S(1)} %and_select_fusion), kind=kOutput, calls=%fused_computation.11 | convolution fusion | flops 35651616 | bytes 12582928 | tf_op jit(solution)/shard_map/ns,slab->lanb/dot_general | solution.py:185
  707.0 3.1 copy.69
  (58 shorter events, 11.2 us)
Async XLA Ops:
  7.2 60.5 %all-gather.9.cloned.1.call-start = ((), (), s32[]{:S(2)}) async-start(), calls=%async_computation.4 | async-start | bytes 2359296 | tf_op jit(solution)/shard_map/all_gather | solution.py:127
  8.9 4.8 slice-start.4
  8.9 186.3 %all-gather.5.cloned.1.call-start = ((), (), s32[]{:S(2)}) async-start(), calls=%async_computation.2 | async-start | bytes 9437184 | tf_op jit(solution)/shard_map/all_gather | solution.py:110
  10.4 1.7 copy-start.1
  10.4 1.7 collective-permute-start
  14.8 55.0 %copy-start.2 = (f32[256,1024]{1,0:T(8,128)S(1)}, f32[256,1024]{1,0:T(8,128)}, u32[]{:S(2)}) copy-start(f32[256,1024]{1,0:T(8,128)} %copy-done.1) | copy-start | bytes 3145732
  14.8 239.1 %all-gather.7.cloned.1.call-start = ((), (), s32[]{:S(2)}) async-start(), calls=%async_computation.3 | async-start | bytes 10485760 | tf_op jit(solution)/shard_map/all_gather | solution.py:129
  69.6 1.7 copy-start
  253.9 126.8 %slice-start = ((s8[8388608]{0:T(1024)(128)(4,1)}), s8[4194304]{0:T(1024)(128)(4,1)S(1)}, s32[]{:S(2)}) async-start(s8[8388608]{0:T(1024)(128)(4,1)} %bitcast.76), calls=%async_computation.5 | async-start | bytes 8388608
  253.9 152.0 %slice-start.2 = ((s8[8388608]{0:T(1024)(128)(4,1)}), s8[4194304]{0:T(1024)(128)(4,1)S(1)}, s32[]{:S(2)}) async-start(s8[8388608]{0:T(1024)(128)(4,1)} %bitcast.79), calls=%async_computation.7 | async-start | bytes 8388608
  256.8 123.9 %slice-start.1 = ((s8[8388608]{0:T(1024)(128)(4,1)}), s8[4194304]{0:T(1024)(128)(4,1)S(1)}, s32[]{:S(2)}) async-start(s8[8388608]{0:T(1024)(128)(4,1)} %bitcast.76), calls=%async_computation.6 | async-start | bytes 8388608
  256.8 149.1 %slice-start.3 = ((s8[8388608]{0:T(1024)(128)(4,1)}), s8[4194304]{0:T(1024)(128)(4,1)S(1)}, s32[]{:S(2)}) async-start(s8[8388608]{0:T(1024)(128)(4,1)} %bitcast.79), calls=%async_computation.8 | async-start | bytes 8388608
  396.5 9.5 %copy-start.3 = (f32[2048,1024]{1,0:T(8,128)S(1)}, f32[2048,1024]{1,0:T(8,128)}, u32[]{:S(2)}) copy-start(f32[2048,1024]{1,0:T(8,128)} %fusion.3) | copy-start | bytes 25165828
  437.3 53.1 %all-to-all-start = ((bf16[8,256,4,256]{3,2,1,0:T(4,128)(2,1)}), bf16[8,256,4,256]{3,2,1,0:T(4,128)(2,1)}, u32[]{:S(2)}, u32[]{:S(2)}) async-start(bf16[8,256,4,256]{3,2,1,0:T(4,128)(2,1)} %copy.57), calls=%async_computation | async-start | bytes 8388608 | tf_op jit(solution)/shard_map/all_to_all | solution.py:177
  509.4 188.7 %all-to-all-start.1 = ((bf16[8,8,256,256]{3,2,1,0:T(8,128)(2,1)}), bf16[8,8,256,256]{3,2,1,0:T(8,128)(2,1)}, u32[]{:S(2)}, u32[]{:S(2)}) async-start(bf16[8,8,256,256]{3,2,1,0:T(8,128)(2,1)} %copy.60), calls=%async_computation.1 | async-start | bytes 16777216 | tf_op jit(solution)/shard_map/all_to_all | solution.py:184
Sparse Core Ops, SparseCore 0:
  10.1 57.4 all-gather.8
  70.3 124.9 all-gather.4
  197.4 56.4 all-gather.6
